TPU v7x, 32 devices: a whole 2x2x4 slice. The times are simulated.
32 devices in a mesh: groups: 2 (over x), dp: 8 (over z, y), owner: 2 (over core).
Axes of the slice: x: 2, y: 2, z: 4, core: 2. Of those that a mesh axis runs over, the one named last changes fastest.
Arguments:
- inputs: bfloat16 [2, 8192, 1408], P('owner', ('groups', 'dp')), parts along dimension 1, may hold values from -6 to 6
- grad_weight: bfloat16 [2816, 1408], P('groups'), parts along dimension 0, may hold values from -6 to 6
- counts: int32 [16], P('groups'), parts along dimension 0, may hold values from 128 to 512
- owners: int32 [4], P('groups'), parts along dimension 0, may hold values from 0 to 7
Outputs:
- kept_inverse: bfloat16 [16, 2, 1408, 1408], P(('groups', 'dp'), 'owner'), parts along dimension 0
- precond: bfloat16 [2816, 1408], P(('groups', 'dp', 'owner')), parts along dimension 0
There are 2 independent parts, one for each index of `groups`. A program takes and returns all parts, laid end to end along the dimension named above; each array names one. Nothing has to cross between parts.
Inputs may be any that keep to these rules, and one draw needn't show every extreme that they name: `counts`: live tokens come first in each shard's slots. Core k of chip owners[k] owns factor k; both factors may have the same chip.
All inputs are finite; a program needn't handle non-finite values.
Results may differ from a plain program's by a relative error of at most 0.0065.
Values may be sent and summed in bfloat16 or wider, within the bound.
No kernel may reach another device: no remote copies, remote signals or barrier semaphores. Data moves between devices by JAX's collectives and lax.ppermute only.
A program may use at most 192 MiB of HBM per device.

v0:
```python
import jax
import jax.numpy as jnp
from jax import lax
from jax.sharding import PartitionSpec as P

damping_term = 0.1


def broadcast(block, axis, holder):
    block = jnp.where(lax.axis_index(axis) == holder, block, jnp.zeros_like(block))
    return lax.psum(block, axis)


def chol_inverse(matrix):
    triangle = jnp.linalg.cholesky(matrix)
    identity = jnp.eye(matrix.shape[0], dtype=jnp.float32)
    return jax.scipy.linalg.cho_solve((triangle, True), identity)


def invert_factor(damped):
    half_width = damped.shape[0] // 2
    upper_left = damped[:half_width, :half_width]
    upper_right = damped[:half_width, half_width:]
    lower_right = damped[half_width:, half_width:]
    best = lax.Precision.HIGHEST
    left_inverse = chol_inverse(upper_left)
    weighted = jnp.dot(left_inverse, upper_right, precision=best)
    schur = lower_right - jnp.dot(upper_right.T, weighted, precision=best)
    schur_inverse = chol_inverse(schur)
    across = jnp.dot(weighted, schur_inverse, precision=best)
    top_left = left_inverse + jnp.dot(across, weighted.T, precision=best)
    top_row = jnp.concatenate([top_left, -across], axis=1)
    bottom_row = jnp.concatenate([-across.T, schur_inverse], axis=1)
    return jnp.concatenate([top_row, bottom_row], axis=0).astype(jnp.bfloat16)


def on_device(inputs, grad_weight, counts, owners):
    samples = inputs[0]
    tok_rows = samples.shape[0]
    features = samples.shape[1]
    chip_index = lax.axis_index("dp")
    core_index = lax.axis_index("owner")
    live_rows = jnp.arange(tok_rows) < counts[chip_index]
    masked = jnp.where(live_rows[:, None], samples, jnp.zeros_like(samples))
    contract = (((0,), (0,)), ((), ()))
    shares = lax.psum_scatter(
        lax.dot_general(masked, samples, contract, preferred_element_type=jnp.float32),
        "dp",
        scatter_dimension=0,
        tiled=True,
    )
    summed = lax.all_gather(shares, "dp", axis=0, tiled=True)
    token_total = jnp.sum(counts).astype(jnp.float32)
    damped = summed / token_total + damping_term * jnp.eye(features, dtype=jnp.float32)
    is_owner = owners[core_index] == chip_index
    blank = jnp.zeros((features, features), jnp.bfloat16)
    row_count = features // (2 * lax.axis_size("dp"))
    row_start = (chip_index * 2 + core_index) * row_count
    inverse = lax.cond(is_owner, invert_factor, lambda matrix: blank, damped)
    builder = jnp.logical_and(is_owner, core_index == 0)
    left_part = lax.cond(
        builder,
        lambda: jnp.dot(grad_weight, inverse, preferred_element_type=jnp.float32).astype(
            jnp.bfloat16
        ),
        lambda: blank,
    )
    left_whole = broadcast(left_part, ("dp", "owner"), owners[0] * 2)
    gradient_inverse = broadcast(inverse, ("dp", "owner"), owners[1] * 2 + 1)
    inverse_rows = lax.dynamic_slice_in_dim(gradient_inverse, row_start, row_count, 0)
    precond = jnp.dot(inverse_rows, left_whole, preferred_element_type=jnp.float32).astype(
        jnp.bfloat16
    )
    return (inverse[None, None], precond)


def solution(mesh):
    return jax.shard_map(
        on_device,
        mesh=mesh,
        in_specs=(P("owner", ("groups", "dp"), None), P("groups", None), P("groups"), P("groups")),
        out_specs=(P(("groups", "dp"), "owner", None, None), P(("groups", "dp", "owner"), None)),
        check_vma=False,
    )
```

profile of v0, /device:TPU:0, one launch (start us, length us, event | category | flops | bytes accessed | tf_op | source)
XLA Modules:
  0.0 1056.9 jit_solution(2252185139663675642)
XLA Ops:
  7.2 0.0 reduce-scatter.2.cloned.1.call-start
  7.2 1.2 dynamic_slice.10
  8.5 0.6 iota_compare_fusion.7
  9.1 7.5 fusion.181
  16.6 0.0 copy-start.22
  16.6 0.0 copy-start.21
  16.6 0.0 reduce-scatter.2.cloned.1.call-update
  16.7 0.0 all-gather.2.cloned.1.call-start
  16.7 144.6 %reduce-scatter.2.cloned.1.call-done = f32[176,1408]{1,0:T(8,128)} async-done(((f32[1408,1408]{1,0:T(8,128)}), f32[176,1408]{1,0:T(8,128)}) %reduce-scatter.2.cloned.1.call-update) | async-done | bytes 991248 | tf_op jit(solution)/shard_map/reduce_scatter | solution.py:46
  161.3 0.0 all-gather.2.cloned.1.call-update
  161.3 0.0 all-reduce.6.cloned.1.call-start
  161.3 0.0 copy-done.22
  161.4 0.6 reduce_sum.9
  162.6 0.0 copy-done.21
  162.6 0.6 fusion.193
  165.2 116.6 %all-gather.2.cloned.1.call-done = f32[1408,1408]{1,0:T(8,128)} async-done(((f32[176,1408]{1,0:T(8,128)}), f32[1408,1408]{1,0:T(8,128)}) %all-gather.2.cloned.1.call-update) | async-done | bytes 7929872 | tf_op jit(solution)/shard_map/all_gather | solution.py:52
  281.8 3.7 iota.133
  285.5 3.7 iota.132
  289.1 6.7 conditional.2
  289.1 2.3 broadcast.234.clone
  291.4 2.2 broadcast_in_dim.16.clone
  293.6 2.3 broadcast.234
  295.9 2.3 conditional.3
  295.9 2.3 broadcast.242
  298.2 3.8 broadcast_select_fusion
  301.9 0.0 all-reduce.6.cloned.1.call-update
  301.9 744.7 %all-reduce.6.cloned.1.call-done = (bf16[1408,1408]{1,0:T(8,128)(2,1)}, bf16[1408,1408]{1,0:T(8,128)(2,1)}) async-done(((bf16[1408,1408]{1,0:T(8,128)(2,1)}, bf16[1408,1408]{1,0:T(8,128)(2,1)}), (bf16[1408,1408]{1,0:T(8,128)(2,1)}, bf16[1408,1408]{1,0:T(8,128)(2,1)})) %all-reduce.6.cloned.1.call-update) | async-done | bytes 7929872 | tf_op jit(solution)/shard_map/psum | solution.py:11
  1046.7 3.7 convolution_convert_fusion.1
Async XLA Ops:
  7.2 154.1 %reduce-scatter.2.cloned.1.call-start = ((), (), s32[]{:S(2)}) async-start(), calls=%async_computation.1 | async-start | bytes 8921088 | tf_op jit(solution)/shard_map/reduce_scatter | solution.py:46
  16.6 144.7 %copy-start.22 = (s32[8]{0:T(128)S(1)}, s32[8]{0:T(128)}, u32[]{:S(2)}) copy-start(s32[8]{0:T(128)} %param.13) | copy-start | bytes 100
  16.6 146.0 %copy-start.21 = (s32[2]{0:T(128)S(1)}, s32[2]{0:T(128)}, u32[]{:S(2)}) copy-start(s32[2]{0:T(128)} %param.14) | copy-start | bytes 28
  16.7 265.1 %all-gather.2.cloned.1.call-start = ((), (), s32[]{:S(2)}) async-start(), calls=%async_computation.2 | async-start | bytes 8921088 | tf_op jit(solution)/shard_map/all_gather | solution.py:52
  161.3 885.4 %all-reduce.6.cloned.1.call-start = ((), (), s32[]{:S(2)}) async-start(), calls=%async_computation.3 | async-start | bytes 15859712 | tf_op jit(solution)/shard_map/psum | solution.py:11
Sparse Core Ops, SparseCore 0:
  16.8 144.4 reduce-scatter.1
  163.5 118.2 all-gather.1
  302.1 744.5 all-reduce.5
where the time goes:
time: 1060 us
  waiting for transfers between devices  1010 us (95%)
  local copies, waits for them, and re-layouts  18.2 us (2%)
  between operations  16.4 us (2%)
  matrix products  11.2 us (1%)
    psum x1, waiting for transfers between devices, broadcast(): return lax.psum(block, axis)  745 us
    reduce_scatter x1, waiting for transfers between devices, on_device(): lax.psum_scatter(lax.dot_general(masked, samples, contract, preferred_ele...  145 us
    all_gather x1, waiting for transfers between devices, on_device(): summed = lax.all_gather(shares, 'dp', axis=0, tiled=True)  117 us
  transfers between devices with their start and end apart: 3, of which 3 were waited for; matrix products, arithmetic and copies ran while one was open for 0% of the time, Pallas kernels for 0%

commit v1 on v0

v1 whole, which is shorter than its diff:
```python
import functools

import jax
import jax.numpy as jnp
from jax import lax
from jax.experimental import pallas as pl
from jax.experimental.pallas import tpu as pltpu
from jax.sharding import PartitionSpec as P

damping_term = 0.1
TILE = 128
f32 = jnp.float32
bf16 = jnp.bfloat16


def split3(x):
    a = x.astype(bf16)
    r = x - a.astype(f32)
    b = r.astype(bf16)
    c = (r - b.astype(f32)).astype(bf16)
    return a, b, c


def left_parts(x):
    a, b, c = split3(x)
    return jnp.concatenate([a, a, b, a, b, c], axis=1)


def right_parts(x):
    a, b, c = split3(x)
    return jnp.concatenate([a, b, a, c, b, a], axis=0)


def mm(a, b):
    return jnp.dot(a, b, preferred_element_type=f32)


def all_rows(x, p):
    return jnp.broadcast_to(x[p : p + 1, :], x.shape)


def tree_sum(xs):
    while len(xs) > 1:
        xs = [xs[i] + xs[i + 1] if i + 1 < len(xs) else xs[i] for i in range(0, len(xs), 2)]
    return xs[0]


def sweep8(M, g):
    n = M.shape[0]
    p0 = 8 * g
    lane = lax.broadcasted_iota(jnp.int32, (8, n), 1)
    sub = lax.broadcasted_iota(jnp.int32, (8, n), 0)
    inside = (lane >= p0) & (lane < p0 + 8)
    R = M[p0 : p0 + 8, :]
    V = [jnp.broadcast_to(R[:, p0 + j : p0 + j + 1], (8, n)) for j in range(8)]
    for p in range(8):
        at = sub == p
        inv = 1.0 / all_rows(V[p], p)
        Vp = jnp.where(at, -1.0, V[p])
        V = [
            Vp * inv if j == p else jnp.where(at, 0.0, V[j]) - Vp * (all_rows(V[j], p) * inv)
            for j in range(8)
        ]
    Rq = jnp.where(inside, jnp.where(lane - p0 == sub, 1.0, 0.0), -R)
    W = tree_sum([V[r] * all_rows(Rq, r) for r in range(8)])
    Wb = [all_rows(W, r) for r in range(8)]
    out = []
    for i in range(n // 8):
        if i == g:
            out.append(W)
            continue
        Mi = M[8 * i : 8 * i + 8, :]
        t = [jnp.broadcast_to(Mi[:, p0 + r : p0 + r + 1], (8, n)) * Wb[r] for r in range(8)]
        out.append(jnp.where(inside, 0.0, Mi) - tree_sum(t))
    return jnp.concatenate(out, axis=0)


def sweep_tile(M):
    for g in range(M.shape[0] // 8):
        M = sweep8(M, g)
    return M


def factor_kernel(count_ref, x_ref, out_ref):
    rows, n = x_ref.shape
    x = x_ref[...]
    live = lax.broadcasted_iota(jnp.int32, (rows, n), 0) < count_ref[0]
    x = jnp.where(live, x, jnp.zeros_like(x))
    xt = x.T
    at = 0
    for i in range(n // TILE):
        row = mm(xt[i * TILE : (i + 1) * TILE, :], x[:, : (i + 1) * TILE])
        for j in range(i + 1):
            out_ref[at : at + TILE, :] = row[:, j * TILE : (j + 1) * TILE]
            at += TILE


def invert_kernel(scale_ref, keep_ref, tiles_ref, inv_ref, kept_ref, A, Cs, Ws, Wf, N):
    n = A.shape[0]
    blocks = n // TILE
    scale = scale_ref[0]
    eye = jnp.where(
        lax.broadcasted_iota(jnp.int32, (TILE, TILE), 0)
        == lax.broadcasted_iota(jnp.int32, (TILE, TILE), 1),
        damping_term,
        0.0,
    )
    at = 0
    for i in range(blocks):
        for j in range(i + 1):
            t = tiles_ref[at : at + TILE, :] * scale
            at += TILE
            if i == j:
                t = t + eye
            A[i * TILE : (i + 1) * TILE, j * TILE : (j + 1) * TILE] = t
            if i != j:
                A[j * TILE : (j + 1) * TILE, i * TILE : (i + 1) * TILE] = t.T
    N[...] = sweep_tile(A[:TILE, :TILE])
    wide = 2 * TILE

    def step(k, _):
        here = pl.ds(pl.multiple_of(k * TILE, TILE), TILE)
        later = pl.ds(pl.multiple_of(jnp.minimum(k + 1, blocks - 1) * TILE, TILE), TILE)
        D = N[...]
        Nl = left_parts(D)
        Nr = right_parts(D)
        for c in range(0, n, wide):
            w = min(wide, n - c)
            Wc = mm(Nl, right_parts(A[here, c : c + w]))
            Wf[:, c : c + w] = Wc
            Ws[:, c : c + w] = right_parts(Wc)
        for r in range(0, n, wide):
            h = min(wide, n - r)
            Cs[r : r + h, :] = left_parts(A[r : r + h, here])
        T = A[later, later] + mm(Cs[later, :], Ws[:, later])
        N[...] = sweep_tile(T)
        for c in range(0, n, wide):
            w = min(wide, n - c)
            A[:, c : c + w] = A[:, c : c + w] + mm(Cs[...], Ws[:, c : c + w])
        A[:, here] = -mm(Cs[...], Nr)
        A[here, :] = -Wf[...]
        A[here, here] = D
        return 0

    lax.fori_loop(0, blocks, step, 0)
    keep = keep_ref[0] != 0
    for i in range(blocks):
        rows = slice(i * TILE, (i + 1) * TILE)
        r = (-A[rows, :]).astype(bf16)
        inv_ref[rows, :] = r
        kept_ref[rows, :] = jnp.where(keep, r, jnp.zeros_like(r))


def vmem():
    return pl.BlockSpec(memory_space=pltpu.VMEM)


def smem():
    return pl.BlockSpec(memory_space=pltpu.SMEM)


def packed_factor(samples, count):
    n = samples.shape[1]
    blocks = n // TILE
    tiles = blocks * (blocks + 1) // 2
    return pl.pallas_call(
        factor_kernel,
        out_shape=jax.ShapeDtypeStruct((tiles * TILE, TILE), f32),
        in_specs=[smem(), vmem()],
        out_specs=vmem(),
        compiler_params=pltpu.CompilerParams(vmem_limit_bytes=48 << 20),
        name="factor_terms",
    )(count, samples)


def invert(tiles, scale, keep, n):
    return pl.pallas_call(
        invert_kernel,
        out_shape=[jax.ShapeDtypeStruct((n, n), bf16)] * 2,
        in_specs=[smem(), smem(), vmem()],
        out_specs=[vmem(), vmem()],
        scratch_shapes=[
            pltpu.VMEM((n, n), f32),
            pltpu.VMEM((n, 6 * TILE), bf16),
            pltpu.VMEM((6 * TILE, n), bf16),
            pltpu.VMEM((TILE, n), f32),
            pltpu.VMEM((TILE, TILE), f32),
        ],
        compiler_params=pltpu.CompilerParams(vmem_limit_bytes=56 << 20),
        name="invert_factor",
    )(scale, keep, tiles)


def on_device(inputs, grad_weight, counts, owners):
    samples = inputs[0]
    n = samples.shape[1]
    chip = lax.axis_index("dp")
    core = lax.axis_index("owner")
    count = lax.dynamic_slice_in_dim(counts, chip, 1)
    terms = packed_factor(samples, count)
    shares = lax.psum_scatter(terms, "dp", scatter_dimension=0, tiled=True)
    summed = lax.all_gather(shares, "dp", axis=0, tiled=True)
    scale = 1.0 / jnp.sum(counts).astype(f32)
    keep = (owners[core] == chip).astype(jnp.int32)
    inverse, kept = invert(summed, scale[None], keep[None], n)
    rows = n // lax.axis_size("dp")
    part = lax.dynamic_slice_in_dim(inverse, chip * rows, rows, 0)
    left = jnp.dot(part, grad_weight, preferred_element_type=f32)
    left = lax.ppermute(left, "owner", [(1, 0)])
    high = left.astype(bf16)
    low = (left - high.astype(f32)).astype(bf16)
    both = mm(high, inverse) + mm(low, inverse)
    both = both.astype(bf16)
    half = rows // 2
    other = lax.ppermute(both[half:], "owner", [(0, 1)])
    precond = jnp.where(core == 0, both[:half], other)
    return (kept[None, None], precond)


def solution(mesh):
    return jax.shard_map(
        on_device,
        mesh=mesh,
        in_specs=(P("owner", ("groups", "dp"), None), P("groups", None), P("groups"), P("groups")),
        out_specs=(P(("groups", "dp"), "owner", None, None), P(("groups", "dp", "owner"), None)),
        check_vma=False,
    )
```

time: 1060 us -> 279 us (0.26)
  waiting for transfers between devices: 1010 us -> 172 us
  Pallas kernels: 0 us -> 77.2 us
  local copies, waits for them, and re-layouts: 18.2 us -> 5.22 us
    psum x1 -> x0, waiting for transfers between devices: 745 us -> none  [broadcast(): return lax.psum(block, axis)]
    pallas_call x0 -> x2, Pallas kernels: none -> 77.2 us  [the longest x1 75.1 us: invert(): pl.pallas_call(invert_kernel, out_shape=[jax.ShapeDtypeStruct((n, n), bf1...]
    reduce_scatter x1, waiting for transfers between devices: 145 us -> 92.7 us  [on_device(): shares = lax.psum_scatter(terms, 'dp', scatter_dimension=0, tiled=True)]
    all_gather x1, waiting for transfers between devices: 117 us -> 74.6 us  [on_device(): summed = lax.all_gather(shares, 'dp', axis=0, tiled=True)]
  transfers between devices with their start and end apart: 3 -> 4, of which waited for: 3 -> 4; matrix products, arithmetic and copies ran while one was open for 0% -> 0% of each run, Pallas kernels for 0% -> 0%
where the time goes in v1:
time: 279 us
  waiting for transfers between devices  172 us (62%)
  Pallas kernels  77.2 us (28%)
  between operations  15.5 us (6%)
  local copies, waits for them, and re-layouts  5.22 us (2%)
  matrix products  4.25 us (2%)
  starting transfers between devices  3.42 us (1%)
    reduce_scatter x1, waiting for transfers between devices, on_device(): shares = lax.psum_scatter(terms, 'dp', scatter_dimension=0, tiled=True)  92.7 us
    pallas_call x1, Pallas kernels, invert(): pl.pallas_call(invert_kernel, out_shape=[jax.ShapeDtypeStruct((n, n), bf1...  75.1 us
    all_gather x1, waiting for transfers between devices, on_device(): summed = lax.all_gather(shares, 'dp', axis=0, tiled=True)  74.6 us
  transfers between devices with their start and end apart: 4, of which 4 were waited for; matrix products, arithmetic and copies ran while one was open for 0% of the time, Pallas kernels for 0%

profile of v1, /device:TPU:0, one launch (start us, length us, event | category | flops | bytes accessed | tf_op | source)
XLA Modules:
  0.0 278.6 jit_solution(8897853132688209658)
XLA Ops:
  7.2 0.0 reduce-scatter.2.cloned.1.call-start
  7.2 1.2 dynamic_slice.10.count_ref
  8.5 0.0 copy-start.1
  8.5 1.4 copy-done.1
  9.8 0.0 copy-start.4
  9.8 0.0 copy-start.5
  9.8 2.1 factor_terms.1
  12.0 0.0 copy-start
  12.0 2.0 copy-done
  14.0 0.0 reduce-scatter.2.cloned.1.call-update
  14.0 0.0 all-gather.2.cloned.1.call-start
  14.1 92.7 %reduce-scatter.2.cloned.1.call-done = f32[1056,128]{1,0:T(8,128)} async-done(((f32[8448,128]{1,0:T(8,128)}), f32[1056,128]{1,0:T(8,128)}) %reduce-scatter.2.cloned.1.call-update) | async-done | bytes 540688 | tf_op jit(solution)/shard_map/reduce_scatter | solution.py:201
  106.8 0.0 all-gather.2.cloned.1.call-update
  106.8 0.0 copy-done.4
  106.8 0.6 reduce_sum.9
  108.1 0.0 copy-done.5
  108.1 0.6 dynamic_slice.9
  109.4 74.6 %all-gather.2.cloned.1.call-done.tiles_ref = f32[8448,128]{1,0:T(8,128)} async-done(((f32[1056,128]{1,0:T(8,128)}), f32[8448,128]{1,0:T(8,128)}) %all-gather.2.cloned.1.call-update) | async-done | bytes 4325392 | tf_op jit(solution)/shard_map/all_gather | solution.py:202
  184.0 0.0 copy-start.3
  184.0 75.1 %invert_factor.1 = (bf16[1408,1408]{1,0:T(8,128)(2,1)}, bf16[1408,1408]{1,0:T(8,128)(2,1)}) custom-call(f32[1]{0:T(128)} %bitcast.scale_ref, s32[1]{0:T(128)} %bitcast.2.keep_ref, f32[8448,128]{1,0:T(8,128)} %all-gather.2.cloned.1.call-done.tiles_ref), custom_call_target="tpu_custom_call" | custom-call | tf_op jit(solution)/shard_map/invert_factor/pallas_call | solution.py:177
  259.1 0.0 copy-start.2
  259.1 0.0 copy-done.3
  259.1 2.2 fusion.2
  261.3 1.3 collective-permute-start
  262.6 3.2 %collective-permute-done = f32[176,1408]{1,0:T(8,128)S(1)} collective-permute-done((f32[176,1408]{1,0:T(8,128)S(1)}, f32[176,1408]{1,0:T(8,128)S(1)}, u32[]{:S(2)}, u32[]{:S(2)}) %collective-permute-start) | collective-permute-done | bytes 991264 | tf_op jit(solution)/shard_map/ppermute | solution.py:209
  265.8 0.0 copy-done.2
  265.8 1.0 fusion.1
  266.8 1.0 fusion
  267.9 2.0 collective-permute-start.1
  269.9 1.1 collective-permute-done.1
  271.0 0.7 slice_select_fusion
  (1 shorter events, 0.0 us)
Async XLA Ops:
  7.2 99.6 %reduce-scatter.2.cloned.1.call-start = ((), (), s32[]{:S(2)}) async-start(), calls=%async_computation.1 | async-start | bytes 4866048 | tf_op jit(solution)/shard_map/reduce_scatter | solution.py:201
  8.5 1.4 copy-start.1
  9.8 97.0 %copy-start.4 = (s32[8]{0:T(128)S(1)}, s32[8]{0:T(128)}, u32[]{:S(2)}) copy-start(s32[8]{0:T(128)} %param.6) | copy-start | bytes 100
  9.8 98.3 %copy-start.5 = (s32[2]{0:T(128)S(1)}, s32[2]{0:T(128)}, u32[]{:S(2)}) copy-start(s32[2]{0:T(128)} %param.7) | copy-start | bytes 28
  12.0 2.0 copy-start
  14.0 170.0 %all-gather.2.cloned.1.call-start = ((), (), s32[]{:S(2)}) async-start(), calls=%async_computation.2 | async-start | bytes 4866048 | tf_op jit(solution)/shard_map/all_gather | solution.py:202
  184.0 75.1 %copy-start.3 = (bf16[1408,1408]{1,0:T(8,128)(2,1)S(1)}, bf16[1408,1408]{1,0:T(8,128)(2,1)}, u32[]{:S(2)}) copy-start(bf16[1408,1408]{1,0:T(8,128)(2,1)} %param.5) | copy-start | bytes 11894788
  259.1 6.7 %copy-start.2 = (bf16[1408,1408]{1,0:T(8,128)(2,1)S(1)}, bf16[1408,1408]{1,0:T(8,128)(2,1)}, u32[]{:S(2)}) copy-start(bf16[1408,1408]{1,0:T(8,128)(2,1)} %get-tuple-element.5) | copy-start | bytes 11894788
  261.3 4.5 %collective-permute-start = (f32[176,1408]{1,0:T(8,128)S(1)}, f32[176,1408]{1,0:T(8,128)S(1)}, u32[]{:S(2)}, u32[]{:S(2)}) collective-permute-start(f32[176,1408]{1,0:T(8,128)S(1)} %fusion.2), channel_id=1, source_target_pairs={{1,0},{3,2},{5,4},{7,6},{9,8},{11,10},{13,12},{15,14},{17,16},{19,... | collective-permute-start | bytes 2973704 | tf_op jit(solution)/shard_map/ppermute | solution.py:209
  267.9 3.2 %collective-permute-start.1 = (bf16[88,1408]{1,0:T(8,128)(2,1)S(1)}, bf16[88,1408]{1,0:T(8,128)(2,1)S(1)}, u32[]{:S(2)}, u32[]{:S(2)}) collective-permute-start(bf16[88,1408]{1,0:T(8,128)(2,1)S(1)} %slice.9), channel_id=1, source_target_pairs={{0,1},{2,3},{4,5},{6,7},{8,9},{10,11},{12,13},{14,15},{16,17},{18,... | collective-permute-start | bytes 743432 | tf_op jit(solution)/shard_map/ppermute | solution.py:215
Sparse Core Ops, SparseCore 0:
  14.1 92.6 reduce-scatter.1
  109.2 74.7 all-gather.1
